TPU v7x, 256 devices: a whole 4x4x8 slice. The times are simulated.
256 devices in a mesh: dom: 32 (over z, y_lo, core), tile: 8 (over y_hi, x).
Axes of the slice: x: 4, y: 4 (y_hi: 2, y_lo: 2; y = y_hi * 2 + y_lo), z: 8, core: 2. Of those that a mesh axis runs over, the one named last changes fastest.
Arguments:
- state: float32 [64, 3, 256, 1024], P('dom', None, 'tile'), may hold values from -6 to 6
- noise: float32 [64, 256, 1024], P('dom', 'tile'), may hold values from -4 to 4
- parents: int32 [64], replicated, may hold values from 0 to 63, as said below
- measured_cell_position: int32 [16384], P('tile'), may hold values from 0 to 262143, as said below
- obs_value: float32 [16384], P('tile'), may hold values from -6 to 6
- obs_precision: float32 [16384], P('tile'), may hold values from 0.3 to 27
Outputs:
- predicted_fields: float32 [64, 3, 256, 1024], P('dom', None, 'tile')
- observation_mismatch: float32 [64], P('dom')
Inputs may be any that keep to these rules, and one draw needn't show every extreme that they name: parents never fall from one new particle to the next; the first is 0 and the last is 63. `measured_cell_position`: entries b * 2048 to (b + 1) * 2048 - 1 lie in rows b * 32 to (b + 1) * 32 - 1, all distinct; the first and last cell of those rows are observed.
All inputs are finite; a program needn't handle non-finite values.
Results may differ from a plain program's by a relative error of at most 0.00002.
Values sent between devices are 32-bit elements; how exact they have to be, the bound alone decides.
A program may use at most 128 MiB of HBM per device.

v0:
```python
import jax
import jax.numpy as jnp
from jax import lax
from jax.sharding import PartitionSpec as P

STEPS = 4


courant = 1.2
coriolis = 0.1
relaxation_gain = 0.3


def extended(block, sides, width):
    for axis, dim in sides:
        count = lax.axis_size(axis)
        forward = [(i, i + 1) for i in range(count - 1)]
        backward = [(target, source) for source, target in forward]
        low = lax.ppermute(
            lax.slice_in_dim(block, block.shape[dim] - width, None, axis=dim), axis, forward
        )
        high = lax.ppermute(lax.slice_in_dim(block, 0, width, axis=dim), axis, backward)
        block = jnp.concatenate([low, block, high], axis=dim)
    return block


def column_diff(field):
    return 0.5 * (jnp.roll(field, -1, -1) - jnp.roll(field, 1, -1))


def row_diff(field):
    return 0.5 * (field[..., 2:, :] - field[..., :-2, :])


def advance(free_elevation, zonal_wind_speed, meridional_wind_speed, gain, target):
    height_one = free_elevation[..., 1:-1, :] - courant * (
        column_diff(zonal_wind_speed)[..., 1:-1, :] + row_diff(meridional_wind_speed)
    )
    eastward_velocity_one = (
        zonal_wind_speed[..., 2:-2, :]
        + coriolis * meridional_wind_speed[..., 2:-2, :]
        - courant * column_diff(height_one)[..., 1:-1, :]
    )
    north_one = (
        meridional_wind_speed[..., 2:-2, :]
        - coriolis * zonal_wind_speed[..., 2:-2, :]
        - courant * row_diff(height_one)
    )
    centre = height_one[..., 1:-1, :]
    height_two = centre + gain[2:-2] * (target[2:-2] - centre)
    return (height_two, eastward_velocity_one, north_one)


def resample(state, parents):
    count = lax.axis_size("dom")
    local_particle_count, fields, rows, cols = state.shape
    particle_pieces = state.reshape(local_particle_count, fields, rows, count, cols // count)
    everyone = lax.all_to_all(particle_pieces, "dom", split_axis=3, concat_axis=0, tiled=True)
    chosen = jnp.take(everyone, parents, axis=0)
    returned = lax.all_to_all(chosen, "dom", split_axis=0, concat_axis=3, tiled=True)
    return returned.reshape(local_particle_count, fields, rows, cols)


def body(state, noise, parents, measured_cell_position, obs_value, obs_precision):
    local_particle_count, fields, rows, cols = state.shape
    strip = lax.axis_index("tile")
    strips = lax.axis_size("tile")
    local_cells = measured_cell_position - strip * (rows * cols)
    gain = (
        jnp.zeros((rows * cols,), jnp.float32)
        .at[local_cells]
        .set(relaxation_gain)
        .reshape(rows, cols)
    )
    target = (
        jnp.zeros((rows * cols,), jnp.float32).at[local_cells].set(obs_value).reshape(rows, cols)
    )
    moved = resample(state, parents)
    free_elevation = moved[:, 0] + noise
    zonal_wind_speed = moved[:, 1]
    meridional_wind_speed = moved[:, 2]
    gain_pad = jnp.pad(gain, ((2, 2), (0, 0)))
    target_pad = jnp.pad(target, ((2, 2), (0, 0)))
    for step in range(STEPS):
        stacked = jnp.stack([free_elevation, zonal_wind_speed, meridional_wind_speed], 1).reshape(
            local_particle_count * 3, rows, cols
        )
        wider = extended(stacked, (("tile", 1),), 2)
        wider = wider.reshape(local_particle_count, 3, rows + 4, cols)
        free_elevation, zonal_wind_speed, meridional_wind_speed = advance(
            wider[:, 0], wider[:, 1], wider[:, 2], gain_pad, target_pad
        )
    predicted_fields = jnp.stack([free_elevation, zonal_wind_speed, meridional_wind_speed], 1)
    seen = free_elevation.reshape(local_particle_count, rows * cols)[:, local_cells]
    partial_sum = jnp.sum(obs_precision[None, :] * (obs_value[None, :] - seen) ** 2, axis=1)
    totals = lax.psum(partial_sum, "tile")
    observation_mismatch = 0.5 * totals / jnp.float32(measured_cell_position.shape[0] * strips)
    return (predicted_fields, observation_mismatch)


def solution(mesh):
    placed = (
        P("dom", None, "tile", None),
        P("dom", "tile", None),
        P(),
        P("tile"),
        P("tile"),
        P("tile"),
    )
    return jax.shard_map(
        body,
        mesh=mesh,
        in_specs=placed,
        out_specs=(P("dom", None, "tile", None), P("dom")),
        check_vma=False,
    )
```

profile of v0, /device:TPU:24, one launch (start us, length us, event | category | flops | bytes accessed | tf_op | source)
XLA Modules:
  0.0 209.3 jit_solution(8605983998620216742)
XLA Ops:
  0.6 3.2 %reshape.67 = f32[2,3,32,32,32]{4,3,2,1,0:T(8,128)} reshape(f32[2,3,32,1024]{3,2,1,0:T(8,128)} %param.6) | data formatting | bytes 1572864 | tf_op jit(solution)/shard_map/reshape | solution.py:57
  3.8 3.7 %copy.93 = f32[2,3,32,32,32]{4,2,1,0,3:T(8,128)S(1)} copy(f32[2,3,32,32,32]{4,3,2,1,0:T(8,128)} %reshape.67) | data formatting | bytes 1572864 | tf_op jit(solution)/shard_map/reshape | solution.py:57
  7.6 2.3 %reshape.117 = f32[32,1,6144]{2,1,0:T(1,128)} reshape(f32[32,2,3,32,32]{4,3,2,1,0:T(8,128)S(1)} %bitcast.109) | data formatting | bytes 1572864
  9.8 10.1 %all-to-all-start = ((f32[32,1,6144]{2,1,0:T(1,128)}), f32[32,1,6144]{2,1,0:T(1,128)S(1)}, u32[]{:S(2)}, u32[]{:S(2)}) async-start(f32[32,1,6144]{2,1,0:T(1,128)} %reshape.117), calls=%async_computation | async-start | bytes 1572864 | tf_op jit(solution)/shard_map/all_to_all | solution.py:58
  20.0 23.3 %all-to-all-done = f32[32,1,6144]{2,1,0:T(1,128)S(1)} async-done(((f32[32,1,6144]{2,1,0:T(1,128)}), f32[32,1,6144]{2,1,0:T(1,128)S(1)}, u32[]{:S(2)}, u32[]{:S(2)}) %all-to-all-start) | async-done | bytes 786464 | tf_op jit(solution)/shard_map/all_to_all | solution.py:58
  43.2 0.5 broadcast.115
  43.7 2.5 %reduce.1 = f32[32,6144]{1,0:T(8,128)S(1)} reduce(f32[32,1,6144]{2,1,0:T(1,128)S(1)} %all-to-all-done, f32[]{:T(128)} %broadcast.115), dimensions={1}, to_apply=%all_to_all.24.reduce_sub_computation | reduce | bytes 1572868 | tf_op jit(solution)/shard_map/all_to_all | solution.py:58
  46.3 2.7 %reshape.118 = f32[32,2,3,32,32]{4,3,2,1,0:T(8,128)} reshape(f32[32,6144]{1,0:T(8,128)S(1)} %reduce.1) | data formatting | bytes 1572864
  48.9 2.6 %gather_fusion = f32[64,3,32,32]{3,2,1,0:T(8,128)S(1)} fusion(f32[64,3,32,32]{3,2,1,0:T(8,128)} %bitcast.108, s32[1024]{0:T(1024)S(1)} %pad_clamp_fusion), kind=kCustom, calls=%fused_computation | custom fusion | bytes 1573120 | tf_op jit(solution)/shard_map/jit(_take)/gather | solution.py:59
  51.6 1.9 fusion.83
  53.5 3.7 %reshape.119 = f32[32,1,6144]{2,1,0:T(1,128)} reshape(f32[64,1,3,32,32]{4,3,2,1,0:T(8,128)} %fusion.83) | data formatting | bytes 1572864
  57.2 4.0 %all-to-all-start.1 = ((f32[32,1,6144]{2,1,0:T(1,128)}), f32[32,1,6144]{2,1,0:T(1,128)S(1)}, u32[]{:S(2)}, u32[]{:S(2)}) async-start(f32[32,1,6144]{2,1,0:T(1,128)} %reshape.119), calls=%async_computation.1 | async-start | bytes 1572864 | tf_op jit(solution)/shard_map/all_to_all | solution.py:60
  61.1 23.4 %all-to-all-done.1 = f32[32,1,6144]{2,1,0:T(1,128)S(1)} async-done(((f32[32,1,6144]{2,1,0:T(1,128)}), f32[32,1,6144]{2,1,0:T(1,128)S(1)}, u32[]{:S(2)}, u32[]{:S(2)}) %all-to-all-start.1) | async-done | bytes 786464 | tf_op jit(solution)/shard_map/all_to_all | solution.py:60
  84.5 3.5 %reduce.2 = f32[32,6144]{1,0:T(8,128)} reduce(f32[32,1,6144]{2,1,0:T(1,128)S(1)} %all-to-all-done.1, f32[]{:T(128)} %broadcast.115), dimensions={1}, to_apply=%all_to_all.28.reduce_sub_computation | reduce | bytes 1572868 | tf_op jit(solution)/shard_map/all_to_all | solution.py:60
  88.1 2.1 %reshape.120 = f32[64,1,3,32,32]{4,3,2,1,0:T(8,128)S(1)} reshape(f32[32,6144]{1,0:T(8,128)} %reduce.2) | data formatting | bytes 1572864
  90.2 3.4 %copy.61 = f32[2,3,32,32,1,32]{5,3,2,1,0,4:T(8,128)} copy(f32[2,3,32,32,1,32]{5,2,1,0,3,4:T(8,128)S(1)} %bitcast.110) | data formatting | bytes 1572864 | tf_op jit(solution)/shard_map/all_to_all | solution.py:60
  93.6 3.0 %reshape.68 = f32[2,3,32,1024]{3,2,1,0:T(8,128)S(1)} reshape(f32[2,3,32,32,1,32]{5,3,2,1,0,4:T(8,128)} %copy.61) | data formatting | bytes 1572864 | tf_op jit(solution)/shard_map/reshape | solution.py:61
  96.8 3.4 %collective-permute-start = (f32[6,2,1024]{2,1,0:T(2,128)S(1)}, f32[6,2,1024]{2,1,0:T(2,128)S(1)}, u32[]{:S(2)}, u32[]{:S(2)}) collective-permute-start(f32[6,2,1024]{2,1,0:T(2,128)S(1)} %get-tuple-element.30), channel_id=1, source_target_pairs={{0,1},{1,2},{2,3},{3,4},{4,5},{5,6},{6,7},{8,9},{9,10},{10,11},{11... | collective-permute-start | bytes 147464 | tf_op jit(solution)/shard_map/ppermute | solution.py:19
  100.2 6.1 %collective-permute-start.1 = (f32[6,2,1024]{2,1,0:T(2,128)S(1)}, f32[6,2,1024]{2,1,0:T(2,128)S(1)}, u32[]{:S(2)}, u32[]{:S(2)}) collective-permute-start(f32[6,2,1024]{2,1,0:T(2,128)S(1)} %get-tuple-element.31), channel_id=1, source_target_pairs={{1,0},{2,1},{3,2},{4,3},{5,4},{6,5},{7,6},{9,8},{10,9},{11,10},{12... | collective-permute-start | bytes 147464 | tf_op jit(solution)/shard_map/ppermute | solution.py:22
  106.3 8.1 %scatter_custom_fusion = f32[32768]{0:T(1024)S(1)} fusion(s32[2048]{0:T(1024)S(1)} %get-tuple-element.11, f32[2048]{0:T(1024)S(1)} %broadcast.62, f32[]{:T(128)} %constant.19.clone.1), kind=kCustom, calls=%fused_computation.116 | custom fusion | bytes 131076 | tf_op jit(solution)/shard_map/scatter | solution.py:72
  114.5 8.1 %scatter_custom_fusion.1 = f32[32768]{0:T(1024)S(1)} fusion(s32[2048]{0:T(1024)S(1)} %get-tuple-element.11, f32[2048]{0:T(1024)S(1)} %copy-done.2, f32[]{:T(128)} %constant.19.clone.1), kind=kCustom, calls=%fused_computation.114 | custom fusion | bytes 131076 | tf_op jit(solution)/shard_map/scatter | solution.py:76
  123.1 0.2 fusion.22
  123.6 0.3 fusion.56
  124.0 1.9 collective-permute-start.2
  126.0 7.5 %collective-permute-start.3 = (f32[6,2,1024]{2,1,0:T(2,128)S(1)}, f32[6,2,1024]{2,1,0:T(2,128)S(1)}, u32[]{:S(2)}, u32[]{:S(2)}) collective-permute-start(f32[6,2,1024]{2,1,0:T(2,128)S(1)} %get-tuple-element.29), channel_id=1, source_target_pairs={{1,0},{2,1},{3,2},{4,3},{5,4},{6,5},{7,6},{9,8},{10,9},{11,10},{12... | collective-permute-start | bytes 147464 | tf_op jit(solution)/shard_map/ppermute | solution.py:22
  133.6 1.6 collective-permute-done.3
  135.3 0.2 pad_maximum_fusion.1
  135.6 0.2 fusion.78
  135.8 0.2 fusion.16
  136.2 0.3 fusion.48
  136.7 1.9 collective-permute-start.4
  138.6 8.1 %collective-permute-start.5 = (f32[6,2,1024]{2,1,0:T(2,128)S(1)}, f32[6,2,1024]{2,1,0:T(2,128)S(1)}, u32[]{:S(2)}, u32[]{:S(2)}) collective-permute-start(f32[6,2,1024]{2,1,0:T(2,128)S(1)} %get-tuple-element.27), channel_id=1, source_target_pairs={{1,0},{2,1},{3,2},{4,3},{5,4},{6,5},{7,6},{9,8},{10,9},{11,10},{12... | collective-permute-start | bytes 147464 | tf_op jit(solution)/shard_map/ppermute | solution.py:22
  146.7 1.5 collective-permute-done.5
  148.2 0.2 pad_maximum_fusion.2
  148.7 0.2 fusion.10
  149.2 0.3 fusion.40
  149.7 1.9 collective-permute-start.6
  151.6 7.9 %collective-permute-start.7 = (f32[6,2,1024]{2,1,0:T(2,128)S(1)}, f32[6,2,1024]{2,1,0:T(2,128)S(1)}, u32[]{:S(2)}, u32[]{:S(2)}) collective-permute-start(f32[6,2,1024]{2,1,0:T(2,128)S(1)} %get-tuple-element.25), channel_id=1, source_target_pairs={{1,0},{2,1},{3,2},{4,3},{5,4},{6,5},{7,6},{9,8},{10,9},{11,10},{12... | collective-permute-start | bytes 147464 | tf_op jit(solution)/shard_map/ppermute | solution.py:22
  159.6 1.6 collective-permute-done.7
  161.2 0.2 pad_maximum_fusion.3
  161.7 0.2 fusion.4
  162.2 0.3 fusion.32
  162.5 8.7 %copy.74 = f32[2,32,1024]{0,2,1:T(8,128)} copy(f32[2,32,1024]{2,1,0:T(8,128)S(1)} %get-tuple-element.43) | data formatting | bytes 524288 | tf_op jit(solution)/shard_map/add | solution.py:50
  171.2 11.2 %gather_fusion.1 = f32[2048,2]{1,0:T(8,128)S(1)} fusion(f32[2,32768]{0,1:T(8,128)} %bitcast.107, s32[2048]{0:T(1024)S(1)} %get-tuple-element.10), kind=kCustom, calls=%fused_computation.1 | custom fusion | bytes 40960 | tf_op jit(solution)/shard_map/gather | solution.py:94
  182.4 0.3 copy.75
  183.0 0.9 copy.76
  183.9 24.9 %psum.7 = f32[2]{0:T(128)S(1)} all-reduce(f32[2]{0:T(128)S(1)} %multiply_reduce_fusion), channel_id=1, replica_groups=mesh['dom'=32,'tile'=8] {'tile'}, use_global_device_ids=true, to_apply=%region_3.4 | all-reduce | flops 2 | bytes 16 | tf_op jit(solution)/shard_map/psum | solution.py:96
  208.8 0.5 broadcast_multiply_fusion
  (57 shorter events, 3.5 us)
Async XLA Ops:
  7.6 12.4 %copy-start.4 = (s32[64]{0:T(128)S(1)}, s32[64]{0:T(128)}, u32[]{:S(2)}) copy-start(s32[64]{0:T(128)} %param.8) | copy-start | bytes 772
  9.8 33.4 %all-to-all-start = ((f32[32,1,6144]{2,1,0:T(1,128)}), f32[32,1,6144]{2,1,0:T(1,128)S(1)}, u32[]{:S(2)}, u32[]{:S(2)}) async-start(f32[32,1,6144]{2,1,0:T(1,128)} %reshape.117), calls=%async_computation | async-start | bytes 1572864 | tf_op jit(solution)/shard_map/all_to_all | solution.py:58
  57.2 27.4 %all-to-all-start.1 = ((f32[32,1,6144]{2,1,0:T(1,128)}), f32[32,1,6144]{2,1,0:T(1,128)S(1)}, u32[]{:S(2)}, u32[]{:S(2)}) async-start(f32[32,1,6144]{2,1,0:T(1,128)} %reshape.119), calls=%async_computation.1 | async-start | bytes 1572864 | tf_op jit(solution)/shard_map/all_to_all | solution.py:60
  93.6 3.0 %copy-start = (f32[2,32,1024]{2,1,0:T(8,128)S(1)}, f32[2,32,1024]{2,1,0:T(8,128)}, u32[]{:S(2)}) copy-start(f32[2,32,1024]{2,1,0:T(8,128)} %param.7) | copy-start | bytes 786436
  93.6 12.7 %copy-start.1 = (s32[2048]{0:T(1024)S(1)}, s32[2048]{0:T(1024)}, u32[]{:S(2)}) copy-start(s32[2048]{0:T(1024)} %param.9) | copy-start | bytes 24580
  93.6 20.8 %copy-start.2 = (f32[2048]{0:T(1024)S(1)}, f32[2048]{0:T(1024)}, u32[]{:S(2)}) copy-start(f32[2048]{0:T(1024)} %param.10) | copy-start | bytes 24580
  96.8 25.8 %collective-permute-start = (f32[6,2,1024]{2,1,0:T(2,128)S(1)}, f32[6,2,1024]{2,1,0:T(2,128)S(1)}, u32[]{:S(2)}, u32[]{:S(2)}) collective-permute-start(f32[6,2,1024]{2,1,0:T(2,128)S(1)} %get-tuple-element.30), channel_id=1, source_target_pairs={{0,1},{1,2},{2,3},{3,4},{4,5},{5,6},{6,7},{8,9},{9,10},{10,11},{11... | collective-permute-start | bytes 147464 | tf_op jit(solution)/shard_map/ppermute | solution.py:19
  100.2 22.4 %collective-permute-start.1 = (f32[6,2,1024]{2,1,0:T(2,128)S(1)}, f32[6,2,1024]{2,1,0:T(2,128)S(1)}, u32[]{:S(2)}, u32[]{:S(2)}) collective-permute-start(f32[6,2,1024]{2,1,0:T(2,128)S(1)} %get-tuple-element.31), channel_id=1, source_target_pairs={{1,0},{2,1},{3,2},{4,3},{5,4},{6,5},{7,6},{9,8},{10,9},{11,10},{12... | collective-permute-start | bytes 147464 | tf_op jit(solution)/shard_map/ppermute | solution.py:22
  124.0 9.6 %collective-permute-start.2 = (f32[6,2,1024]{2,1,0:T(2,128)S(1)}, f32[6,2,1024]{2,1,0:T(2,128)S(1)}, u32[]{:S(2)}, u32[]{:S(2)}) collective-permute-start(f32[6,2,1024]{2,1,0:T(2,128)S(1)} %get-tuple-element.28), channel_id=1, source_target_pairs={{0,1},{1,2},{2,3},{3,4},{4,5},{5,6},{6,7},{8,9},{9,10},{10,11},{11... | collective-permute-start | bytes 147464 | tf_op jit(solution)/shard_map/ppermute | solution.py:19
  126.0 9.3 %collective-permute-start.3 = (f32[6,2,1024]{2,1,0:T(2,128)S(1)}, f32[6,2,1024]{2,1,0:T(2,128)S(1)}, u32[]{:S(2)}, u32[]{:S(2)}) collective-permute-start(f32[6,2,1024]{2,1,0:T(2,128)S(1)} %get-tuple-element.29), channel_id=1, source_target_pairs={{1,0},{2,1},{3,2},{4,3},{5,4},{6,5},{7,6},{9,8},{10,9},{11,10},{12... | collective-permute-start | bytes 147464 | tf_op jit(solution)/shard_map/ppermute | solution.py:22
  136.7 10.0 %collective-permute-start.4 = (f32[6,2,1024]{2,1,0:T(2,128)S(1)}, f32[6,2,1024]{2,1,0:T(2,128)S(1)}, u32[]{:S(2)}, u32[]{:S(2)}) collective-permute-start(f32[6,2,1024]{2,1,0:T(2,128)S(1)} %get-tuple-element.26), channel_id=1, source_target_pairs={{0,1},{1,2},{2,3},{3,4},{4,5},{5,6},{6,7},{8,9},{9,10},{10,11},{11... | collective-permute-start | bytes 147464 | tf_op jit(solution)/shard_map/ppermute | solution.py:19
  138.6 9.6 %collective-permute-start.5 = (f32[6,2,1024]{2,1,0:T(2,128)S(1)}, f32[6,2,1024]{2,1,0:T(2,128)S(1)}, u32[]{:S(2)}, u32[]{:S(2)}) collective-permute-start(f32[6,2,1024]{2,1,0:T(2,128)S(1)} %get-tuple-element.27), channel_id=1, source_target_pairs={{1,0},{2,1},{3,2},{4,3},{5,4},{6,5},{7,6},{9,8},{10,9},{11,10},{12... | collective-permute-start | bytes 147464 | tf_op jit(solution)/shard_map/ppermute | solution.py:22
  149.7 9.9 %collective-permute-start.6 = (f32[6,2,1024]{2,1,0:T(2,128)S(1)}, f32[6,2,1024]{2,1,0:T(2,128)S(1)}, u32[]{:S(2)}, u32[]{:S(2)}) collective-permute-start(f32[6,2,1024]{2,1,0:T(2,128)S(1)} %get-tuple-element.24), channel_id=1, source_target_pairs={{0,1},{1,2},{2,3},{3,4},{4,5},{5,6},{6,7},{8,9},{9,10},{10,11},{11... | collective-permute-start | bytes 147464 | tf_op jit(solution)/shard_map/ppermute | solution.py:19
  151.6 9.6 %collective-permute-start.7 = (f32[6,2,1024]{2,1,0:T(2,128)S(1)}, f32[6,2,1024]{2,1,0:T(2,128)S(1)}, u32[]{:S(2)}, u32[]{:S(2)}) collective-permute-start(f32[6,2,1024]{2,1,0:T(2,128)S(1)} %get-tuple-element.25), channel_id=1, source_target_pairs={{1,0},{2,1},{3,2},{4,3},{5,4},{6,5},{7,6},{9,8},{10,9},{11,10},{12... | collective-permute-start | bytes 147464 | tf_op jit(solution)/shard_map/ppermute | solution.py:22
  162.4 20.3 %copy-start.3 = (f32[2048]{0:T(1024)S(1)}, f32[2048]{0:T(1024)}, u32[]{:S(2)}) copy-start(f32[2048]{0:T(1024)} %param.11) | copy-start | bytes 24580
where the time goes:
time: 210 us; the launch traced here: 209 us
  local copies, waits for them, and re-layouts  67.3 us (32%)
  starting transfers between devices  52.8 us (25%)
  waiting for transfers between devices  51.6 us (25%)
  blocking collectives  24.9 us (12%)
  other arithmetic  11.6 us (6%)
    ppermute x4, starting transfers between devices, extended(): lax.ppermute(lax.slice_in_dim(block, 0, width, axis=dim), axis, backward)  29.5 us
    psum x1, blocking collectives, body(): totals = lax.psum(partial_sum, 'tile')  24.9 us
    all_to_all x1, waiting for transfers between devices, resample(): lax.all_to_all(chosen, 'dom', split_axis=0, concat_axis=3, tiled=True)  23.4 us
    all_to_all x1, waiting for transfers between devices, resample(): lax.all_to_all(particle_pieces, 'dom', split_axis=3, concat_axis=0, tiled...  23.3 us
    unnamed x15, local copies, waits for them, and re-layouts  11.7 us
    gather x2, local copies, waits for them, and re-layouts, body(): free_elevation.reshape(local_particle_count, rows * cols)[:, local_cells]  11.6 us
    all_to_all x1, starting transfers between devices, resample(): lax.all_to_all(particle_pieces, 'dom', split_axis=3, concat_axis=0, tiled...  10.1 us
    ppermute x4, starting transfers between devices, extended(): lax.ppermute(lax.slice_in_dim(block, block.shape[dim] - width, None, axis...  9.16 us
  transfers between devices with their start and end apart: 10, of which 7 were waited for; matrix products, arithmetic and copies ran while one was open for 8% of the time, Pallas kernels for 0%

commit v1 on v0

v1 whole, which is shorter than its diff:
```python
import functools

import jax
import jax.numpy as jnp
from jax import lax
from jax.experimental import pallas as pl
from jax.experimental.pallas import tpu as pltpu
from jax.sharding import PartitionSpec as P

STEPS = 4
LANES = 128
HALO = 8
TALL = 48

COURANT = 1.2
CORIOLIS = 0.1
RELAXATION = 0.3

NOISE, GAIN, FIRST, SECOND = range(4)


def split_three(x):
    high = x.astype(jnp.bfloat16)
    rest = x - high.astype(jnp.float32)
    middle = rest.astype(jnp.bfloat16)
    low = (rest - middle.astype(jnp.float32)).astype(jnp.bfloat16)
    return high, middle, low


def kernel(
    n, tiles, cols, obs, obs_all,
    parents, position, value, precision, state, noise,
    fields_out, mismatch_out,
    every0, every1, every2, pick0, pick1, pick2, fields, noise_all, nudge, weight, row_values, work, result, sums,
    spread_send, spread_recv, local_sem, back_send, back_recv, halo_send, halo_recv, sums_send, sums_recv, out_sem,
):
    every = (every0, every1, every2)
    pick = (pick0, pick1, pick2)
    groups = cols // LANES
    dom = lax.axis_index("dom")
    tile = lax.axis_index("tile")
    has_above = tile > 0
    has_below = tile < tiles - 1

    def place(stage, j):
        column = pl.multiple_of((j % groups) * LANES, LANES)
        if stage == 0:
            field, row = j // (2 * groups), 3 * ((j // groups) % 2)
        elif stage == 1:
            field, row = 2, j // groups
        else:
            field, row = j // (2 * groups), 1 + (j // groups) % 2
        return field, row * 8, column

    def partner(i):
        planes = n // 4
        turn = i // 4
        away = (turn + 1) // 2
        ahead = jnp.where(turn % 2 == 1, away, planes - away)
        z = (dom // 4 + ahead) % planes
        return z * 4 + (dom % 4 + i % 4) % 4

    barrier = pltpu.get_barrier_semaphore()

    @pl.loop(1, n)
    def _(i):
        pl.semaphore_signal(barrier, 1, device_id={"dom": (dom + i) % n})

    @pl.loop(1, tiles)
    def _(i):
        pl.semaphore_signal(barrier, 1, device_id={"tile": (tile + i) % tiles})

    noise_copy = pltpu.make_async_copy(noise, noise_all.at[:, HALO:HALO + 32, :], local_sem.at[0])
    noise_copy.start()
    pl.semaphore_wait(barrier, n - 1 + tiles - 1)

    def spread(stage):
        def piece(j):
            field, row, column = place(stage, j)
            return state.at[:, field, pl.ds(pl.multiple_of(row, 8), 8), pl.ds(column, LANES)]

        mine = every[stage].at[pl.ds(2 * dom, 2)]

        @pl.loop(1, n)
        def _(i):
            target = partner(i)
            pltpu.make_async_remote_copy(
                piece(target), mine, spread_send.at[stage], spread_recv.at[stage], device_id={"dom": target}
            ).start()

        pltpu.make_async_copy(piece(dom), mine, spread_recv.at[stage]).start()

    def give_back(stage, first, count, sem):
        field, row, column = place(stage, dom)
        rows, lanes = pl.ds(pl.multiple_of(row, 8), 8), pl.ds(column, LANES)
        rows = pl.ds(pl.multiple_of(HALO + row, 8), 8)
        there = fields.at[pl.ds(first, count), field, rows, lanes]

        @pl.loop(1, n)
        def _(i):
            target = partner(i)
            pltpu.make_async_remote_copy(
                pick[stage].at[pl.ds(2 * target + first, count)], there,
                back_send.at[sem], back_recv.at[sem], device_id={"dom": target},
            ).start()

        pltpu.make_async_copy(pick[stage].at[pl.ds(2 * dom + first, count)], there, back_recv.at[sem]).start()

    def choose(stage):
        pltpu.make_async_copy(every[stage], every[stage], spread_recv.at[stage]).wait()

        @pl.loop(0, 2 * n, unroll=8)
        def _(s):
            pick[stage][s] = every[stage][parents[s]]

    def await_back(sem, count):
        whole = pick[0].at[pl.ds(0, count * n)]
        pltpu.make_async_copy(whole, whole, back_recv.at[sem]).wait()

    def to_above(kind, source, there):
        return pltpu.make_async_remote_copy(
            source, there, halo_send.at[kind, 0], halo_recv.at[kind, 0], device_id={"tile": jnp.maximum(tile - 1, 0)}
        )

    def to_below(kind, source, there):
        return pltpu.make_async_remote_copy(
            source, there, halo_send.at[kind, 1], halo_recv.at[kind, 1],
            device_id={"tile": jnp.minimum(tile + 1, tiles - 1)},
        )

    top, bottom = pl.ds(HALO, HALO), pl.ds(HALO + 24, HALO)
    over, under = pl.ds(0, HALO), pl.ds(HALO + 32, HALO)

    def halos(kind):
        if kind == NOISE:
            up = to_above(kind, noise.at[:, pl.ds(0, HALO), :], noise_all.at[:, under, :])
            down = to_below(kind, noise.at[:, pl.ds(24, HALO), :], noise_all.at[:, over, :])
        elif kind == GAIN:
            up = to_above(kind, nudge.at[:, top, :], nudge.at[:, under, :])
            down = to_below(kind, nudge.at[:, bottom, :], nudge.at[:, over, :])
        else:
            which = pl.ds(0, 2) if kind == FIRST else pl.ds(2, 1)
            up = to_above(kind, fields.at[:, which, top, :], fields.at[:, which, under, :])
            down = to_below(kind, fields.at[:, which, bottom, :], fields.at[:, which, over, :])
        return up, down

    def send_halo(kind):
        up, down = halos(kind)

        @pl.when(has_above)
        def _():
            up.start()

        @pl.when(has_below)
        def _():
            down.start()

    def await_halo(kind):
        up, down = halos(kind)

        @pl.when(has_below)
        def _():
            up.wait_recv()

        @pl.when(has_above)
        def _():
            down.wait_recv()

    def await_halo_sent(kind):
        up, down = halos(kind)

        @pl.when(has_above)
        def _():
            up.wait_send()

        @pl.when(has_below)
        def _():
            down.wait_send()

    spread(0)
    spread(1)
    send_halo(NOISE)

    @pl.when(tile == 0)
    def _():
        fields[:, :, 0:HALO, :] = jnp.zeros((2, 3, HALO, cols), jnp.float32)
        noise_all[:, 0:HALO, :] = jnp.zeros((2, HALO, cols), jnp.float32)
        nudge[:, 0:HALO, :] = jnp.zeros((2, HALO, cols), jnp.float32)

    @pl.when(tile == tiles - 1)
    def _():
        fields[:, :, HALO + 32:, :] = jnp.zeros((2, 3, HALO, cols), jnp.float32)
        noise_all[:, HALO + 32:, :] = jnp.zeros((2, HALO, cols), jnp.float32)
        nudge[:, HALO + 32:, :] = jnp.zeros((2, HALO, cols), jnp.float32)

    local = position[...] - tile * (32 * cols)
    row_of = local // cols
    column_of = local % cols
    in_row = lax.broadcasted_iota(jnp.int32, (32, obs), 0) == row_of

    def put(slot, row):
        spread_row = jnp.where(in_row, row.astype(jnp.float32), 0.0)
        row_values[slot * 32:(slot + 1) * 32, :] = spread_row.astype(jnp.bfloat16)

    put(0, jnp.ones((1, obs), jnp.float32))
    for at, part in enumerate(split_three(value[...])):
        put(1 + at, part)
    for at, part in enumerate(split_three(precision[...])):
        put(4 + at, part)

    wide = min(cols, 256)

    @pl.loop(0, cols // wide)
    def _(block):
        first = pl.multiple_of(block * wide, wide)
        column = lax.broadcasted_iota(jnp.int32, (wide, obs), 0) + first
        in_column = jnp.where(column == column_of, 1.0, 0.0).astype(jnp.bfloat16)
        grid = lax.dot_general(
            row_values[...], in_column, (((1,), (1,)), ((), ())), preferred_element_type=jnp.float32
        )
        lanes = pl.ds(first, wide)
        nudge[0, HALO:HALO + 32, lanes] = RELAXATION * grid[0:32]
        nudge[1, HALO:HALO + 32, lanes] = (grid[32:64] + grid[64:96]) + grid[96:128]
        weight[:, lanes] = (grid[128:160] + grid[160:192]) + grid[192:224]

    send_halo(GAIN)

    choose(0)
    give_back(0, 0, 2, 0)
    spread(2)
    choose(1)
    give_back(1, 0, 2, 1)
    await_back(0, 2)
    send_halo(FIRST)
    choose(2)
    give_back(2, 0, 1, 2)
    give_back(2, 1, 1, 3)
    await_back(1, 2)
    send_halo(SECOND)

    noise_copy.wait()
    for kind in range(4):
        await_halo(kind)

    row_id = lax.broadcasted_iota(jnp.int32, (TALL, cols), 0)
    inside = jnp.logical_and(
        jnp.logical_or(row_id >= HALO, has_above), jnp.logical_or(row_id < HALO + 32, has_below)
    )

    def column_change(a):
        return pltpu.roll(a, cols - 1, 1) - pltpu.roll(a, 1, 1)

    def row_change(a):
        return pltpu.roll(a, TALL - 1, 0) - pltpu.roll(a, 1, 0)

    half = 0.5 * COURANT

    def forecast(p):
        for step in range(STEPS):
            if step == 0:
                h, u, v = fields[p, 0] + noise_all[p], fields[p, 1], fields[p, 2]
            else:
                h, u, v = work[0], work[1], work[2]
            h1 = h - half * (column_change(u) + row_change(v))
            u1 = u + CORIOLIS * v - half * column_change(h1)
            v1 = v - CORIOLIS * u - half * row_change(h1)
            h2 = h1 + nudge[0] * (nudge[1] - h1)
            if step < STEPS - 1:
                work[0] = jnp.where(inside, h2, 0.0)
                work[1] = jnp.where(inside, u1, 0.0)
                work[2] = jnp.where(inside, v1, 0.0)
            else:
                h2 = h2[HALO:HALO + 32]
                result[p, 0] = h2
                result[p, 1] = u1[HALO:HALO + 32]
                result[p, 2] = v1[HALO:HALO + 32]
                miss = nudge[1, HALO:HALO + 32, :] - h2
                miss = weight[...] * (miss * miss)
                total = jnp.zeros((8, LANES), jnp.float32)
                for r in range(4):
                    for c in range(groups):
                        total = total + miss[8 * r:8 * r + 8, LANES * c:LANES * (c + 1)]
                sums[tile, p] = total
        pltpu.make_async_copy(result.at[p], fields_out.at[p], out_sem.at[p]).start()

    await_back(2, 1)
    forecast(0)
    await_back(3, 1)
    forecast(1)

    @pl.loop(1, tiles)
    def _(i):
        pltpu.make_async_remote_copy(
            sums.at[tile], sums.at[tile], sums_send, sums_recv, device_id={"tile": (tile + i) % tiles}
        ).start()

    others = sums.at[pl.ds(0, tiles - 1)]
    pltpu.make_async_copy(others, others, sums_recv).wait()
    total = sums[0]
    for t in range(1, tiles):
        total = total + sums[t]
    for p in range(2):
        mismatch_out[p] = 0.5 * jnp.sum(total[p]) / jnp.float32(obs_all)

    for p in range(2):
        pltpu.make_async_copy(result.at[p], fields_out.at[p], out_sem.at[p]).wait()
    pltpu.make_async_copy(others, others, sums_send).wait()
    two = pick[0].at[pl.ds(0, 2 * (n - 1))]
    one = pick[0].at[pl.ds(0, n - 1)]
    for stage in range(3):
        pltpu.make_async_copy(two, two, spread_send.at[stage]).wait()
    for sem in range(4):
        sent = two if sem < 2 else one
        pltpu.make_async_copy(sent, sent, back_send.at[sem]).wait()
    for kind in range(4):
        await_halo_sent(kind)


def body(state, noise, parents, measured_cell_position, obs_value, obs_precision):
    n, tiles = lax.axis_size("dom"), lax.axis_size("tile")
    cols = state.shape[3]
    obs = measured_cell_position.shape[0]
    f32 = jnp.float32
    vmem = pl.BlockSpec(memory_space=pltpu.VMEM)
    smem = pl.BlockSpec(memory_space=pltpu.SMEM)
    hbm = pl.BlockSpec(memory_space=pl.ANY)
    dma = pltpu.SemaphoreType.DMA
    pieces = pltpu.VMEM((2 * n, 8, LANES), f32)
    return pl.pallas_call(
        functools.partial(kernel, n, tiles, cols, obs, obs * tiles),
        out_shape=(
            jax.ShapeDtypeStruct(state.shape, f32),
            jax.ShapeDtypeStruct((2,), f32),
        ),
        in_specs=[smem, vmem, vmem, vmem, hbm, hbm],
        out_specs=(hbm, smem),
        scratch_shapes=[
            pieces, pieces, pieces, pieces, pieces, pieces,
            pltpu.VMEM((2, 3, TALL, cols), f32),
            pltpu.VMEM((2, TALL, cols), f32),
            pltpu.VMEM((2, TALL, cols), f32),
            pltpu.VMEM((32, cols), f32),
            pltpu.VMEM((7 * 32, obs), jnp.bfloat16),
            pltpu.VMEM((3, TALL, cols), f32),
            pltpu.VMEM((2, 3, 32, cols), f32),
            pltpu.VMEM((tiles, 2, 8, LANES), f32),
            dma((3,)), dma((3,)), dma((1,)), dma((4,)), dma((4,)),
            dma((4, 2)), dma((4, 2)), dma, dma, dma((2,)),
        ],
        compiler_params=pltpu.CompilerParams(
            collective_id=0, has_side_effects=True, vmem_limit_bytes=48 * 1024 * 1024
        ),
    )(
        parents,
        measured_cell_position.reshape(1, obs),
        obs_value.reshape(1, obs),
        obs_precision.reshape(1, obs),
        state,
        noise,
    )


def solution(mesh):
    placed = (
        P("dom", None, "tile", None),
        P("dom", "tile", None),
        P(),
        P("tile"),
        P("tile"),
        P("tile"),
    )
    return jax.shard_map(
        body,
        mesh=mesh,
        in_specs=placed,
        out_specs=(P("dom", None, "tile", None), P("dom")),
        check_vma=False,
    )
```

time: 210 us -> 64.1 us (0.31)
  the two profiles are of different devices: /device:TPU:24 before, /device:TPU:1 now
where the time goes in v1:
time: 64.1 us; the launch traced here: 63.9 us
  Pallas kernels  57 us (89%)
  local copies, waits for them, and re-layouts  6.21 us (10%)
  between operations  0.65 us (1%)
    pallas_call x1, Pallas kernels, body(): pl.pallas_call(functools.partial(kernel, n, tiles, cols, obs, obs * tiles...  57 us
    unnamed x14, local copies, waits for them, and re-layouts  6.21 us

profile of v1, /device:TPU:1, one launch (start us, length us, event | category | flops | bytes accessed | tf_op | source)
XLA Modules:
  0.0 63.9 jit_solution(7443243414069574483)
XLA Ops:
  0.6 0.0 copy-start.5
  0.6 0.6 %copy-done.5 = s32[64]{0:T(128)S(1)} copy-done((s32[64]{0:T(128)S(1)}, s32[64]{0:T(128)}, u32[]{:S(2)}) %copy-start.5) | copy-done | bytes 280
  1.3 0.0 copy-start
  1.3 1.1 %copy-done = f32[2,3,32,1024]{3,2,1,0:T(8,128)S(1)} copy-done((f32[2,3,32,1024]{3,2,1,0:T(8,128)S(1)}, f32[2,3,32,1024]{3,2,1,0:T(8,128)}, u32[]{:S(2)}) %copy-start) | copy-done | bytes 786456
  2.4 0.0 copy-start.1
  2.4 0.9 %copy-done.1 = f32[2,32,1024]{2,1,0:T(8,128)S(1)} copy-done((f32[2,32,1024]{2,1,0:T(8,128)S(1)}, f32[2,32,1024]{2,1,0:T(8,128)}, u32[]{:S(2)}) %copy-start.1) | copy-done | bytes 262168
  3.4 0.0 copy-start.2
  3.4 0.7 %copy-done.2 = s32[2048]{0:T(1024)S(1)} copy-done((s32[2048]{0:T(1024)S(1)}, s32[2048]{0:T(1024)}, u32[]{:S(2)}) %copy-start.2) | copy-done | bytes 8216
  4.1 0.0 copy-start.3
  4.1 0.7 %copy-done.3 = f32[2048]{0:T(1024)S(1)} copy-done((f32[2048]{0:T(1024)S(1)}, f32[2048]{0:T(1024)}, u32[]{:S(2)}) %copy-start.3) | copy-done | bytes 8216
  4.8 0.0 copy-start.4
  4.8 0.7 %copy-done.4 = f32[2048]{0:T(1024)S(1)} copy-done((f32[2048]{0:T(1024)S(1)}, f32[2048]{0:T(1024)}, u32[]{:S(2)}) %copy-start.4) | copy-done | bytes 8216
  5.5 57.0 %shard_map.77 = (f32[2,3,32,1024]{3,2,1,0:T(8,128)S(1)}, f32[2]{0:T(128)S(1)}) custom-call(s32[64]{0:T(128)S(1)} %copy-done.5, s32[1,2048]{1,0:T(1,128)S(1)} %bitcast.3, f32[1,2048]{1,0:T(1,128)S(1)} %bitcast.4, f32[1,2048]{1,0:T(1,128)S(1)} %bitcast.5, f32[2,3,32,1024]{3,2,1,0:T(8,128)S(1)} %copy-done, f32[2,32,1024]{2,1,0:T(8,128)S(1)} %copy-done.1), custom_call_target="tpu_custom_call" | custom-call | tf_op jit(solution)/shard_map/pallas_call | solution.py:329
  62.5 0.9 %copy.10 = f32[2,3,32,1024]{3,2,1,0:T(8,128)} copy(f32[2,3,32,1024]{3,2,1,0:T(8,128)S(1)} %get-tuple-element.4) | data formatting | bytes 1572864
  63.3 0.5 copy.11
Async XLA Ops:
  0.6 0.7 %copy-start.5 = (s32[64]{0:T(128)S(1)}, s32[64]{0:T(128)}, u32[]{:S(2)}) copy-start(s32[64]{0:T(128)} %parents.1) | copy-start | bytes 772
  1.3 1.1 %copy-start = (f32[2,3,32,1024]{3,2,1,0:T(8,128)S(1)}, f32[2,3,32,1024]{3,2,1,0:T(8,128)}, u32[]{:S(2)}) copy-start(f32[2,3,32,1024]{3,2,1,0:T(8,128)} %state.1) | copy-start | bytes 2359300
  2.4 0.9 %copy-start.1 = (f32[2,32,1024]{2,1,0:T(8,128)S(1)}, f32[2,32,1024]{2,1,0:T(8,128)}, u32[]{:S(2)}) copy-start(f32[2,32,1024]{2,1,0:T(8,128)} %noise.1) | copy-start | bytes 786436
  3.4 0.7 %copy-start.2 = (s32[2048]{0:T(1024)S(1)}, s32[2048]{0:T(1024)}, u32[]{:S(2)}) copy-start(s32[2048]{0:T(1024)} %param.9) | copy-start | bytes 24580
  4.1 0.7 %copy-start.3 = (f32[2048]{0:T(1024)S(1)}, f32[2048]{0:T(1024)}, u32[]{:S(2)}) copy-start(f32[2048]{0:T(1024)} %param.10) | copy-start | bytes 24580
  4.8 0.7 %copy-start.4 = (f32[2048]{0:T(1024)S(1)}, f32[2048]{0:T(1024)}, u32[]{:S(2)}) copy-start(f32[2048]{0:T(1024)} %param.11) | copy-start | bytes 24580
